TPU v7x, 512 devices: a whole 4x8x8 slice. The times are simulated.
512 devices in a mesh: shot: 16 (over y_lo, x), space: 32 (over z, y_hi, core).
Axes of the slice: x: 4, y: 8 (y_hi: 2, y_lo: 4; y = y_hi * 4 + y_lo), z: 8, core: 2. Of those that a mesh axis runs over, the one named last changes fastest.
Arguments:
- courant: float32 [512, 256, 128], P('shot', 'space'), may hold values from 0.05 to 0.18
- anchor: int32 [16, 2], P('shot'), may hold values from 0 to 384, as said below
- source: int32 [16, 3], P('shot'), may hold values from 0 to 127, as said below
- wavelet: float32 [16, 3], P('shot'), may hold values from -12 to 12
- receivers: int32 [16, 64, 3], P('shot'), may hold values from 0 to 127, as said below
- observed: float32 [16, 3, 64], P('shot'), may hold values from -3 to 3
- wave_before: float32 [16, 128, 128, 128], P('shot', 'space'), may hold values from -1.8 to 1.8
- wave_now: float32 [16, 128, 128, 128], P('shot', 'space'), may hold values from -1.8 to 1.8
- adjoint_after: float32 [16, 128, 128, 128], P('shot', 'space'), may hold values from -1.8 to 1.8
- adjoint_now: float32 [16, 128, 128, 128], P('shot', 'space'), may hold values from -1.8 to 1.8
Outputs:
- gradient: float32 [512, 256, 128], P('shot', 'space')
Inputs may be any that keep to these rules, and one draw needn't show every extreme that they name: anchor[s] = (ox, oy) with ox at most 384 and oy at most 128; in each column some shot group has 0 and some the column's largest allowed value. `source`: a cell of the aperture: first coordinate below 128, second below 128, third below 128; in each column some shot group has 0 and some the largest value. `receivers`: cells of the aperture: first coordinate below 128, second below 128, third below 128; cells may repeat; in each column some receiver has 0 and some the largest value.
All inputs are finite; a program needn't handle non-finite values.
Results may differ from a plain program's by a relative error of at most 0.00002.
Values sent between devices are 32-bit elements; how exact they have to be, the bound alone decides.
A program may use at most 64 MiB of HBM per device.

v0:
```python
import jax
import jax.numpy as jnp
from jax import lax
from jax.sharding import PartitionSpec as P

STEPS = 3
stencil_coef = (-205.0 / 72.0, 8.0 / 5.0, -1.0 / 5.0, 8.0 / 315.0, -1.0 / 560.0)


def with_halo(cells, sides, width):
    for axis, dim in sides:
        count = lax.axis_size(axis)
        ends = count - 1
        head = lax.slice_in_dim(cells, 0, width, axis=dim)
        tail = lax.slice_in_dim(cells, cells.shape[dim] - width, cells.shape[dim], axis=dim)
        cells = jnp.concatenate(
            [
                lax.ppermute(tail, axis, [(i, (i + 1) % count) for i in range(ends)]),
                cells,
                lax.ppermute(head, axis, [((i + 1) % count, i) for i in range(ends)]),
            ],
            axis=dim,
        )
    return cells


def stencil(padded, extent_x, extent_y, extent_z):

    def offset_view(shift_x, shift_y, shift_z):
        return padded[
            4 + shift_x : 4 + shift_x + extent_x,
            4 + shift_y : 4 + shift_y + extent_y,
            4 + shift_z : 4 + shift_z + extent_z,
        ]

    total = 3.0 * stencil_coef[0] * offset_view(0, 0, 0)
    for reach in range(1, 5):
        beside_all = offset_view(reach, 0, 0) + offset_view(-reach, 0, 0)
        beside_all = beside_all + offset_view(0, reach, 0) + offset_view(0, -reach, 0)
        beside_all = beside_all + offset_view(0, 0, reach) + offset_view(0, 0, -reach)
        total = total + stencil_coef[reach] * beside_all
    return total


def side_pad(extended):
    return jnp.pad(extended, ((0, 0), (4, 4), (4, 4)))


def on_device(
    courant,
    anchor,
    source,
    wavelet,
    receivers,
    observed,
    wave_before,
    wave_now,
    adjoint_after,
    adjoint_now,
):
    block_rows = wave_now.shape[1]
    col_count = wave_now.shape[2]
    depth_count = wave_now.shape[3]
    space_count = lax.axis_size("space")
    start_row = lax.axis_index("space") * block_rows
    corner_x = anchor[0, 0]
    corner_y = anchor[0, 1]
    all_rows = lax.all_gather(courant, "shot", axis=0, tiled=True)
    window = lax.dynamic_slice_in_dim(all_rows, corner_x, block_rows * space_count, 0)
    columns = lax.all_to_all(window, "space", split_axis=0, concat_axis=1, tiled=True)
    speed_window = lax.dynamic_slice_in_dim(columns, corner_y, col_count, 1)
    source_row = source[0, 0] - start_row
    source_inside = (source_row >= 0) & (source_row < block_rows)
    source_clip = jnp.clip(source_row, 0, block_rows - 1)
    receiver_row = receivers[0, :, 0] - start_row
    receiver_inside = (receiver_row >= 0) & (receiver_row < block_rows)
    receiver_flat = (
        jnp.clip(receiver_row, 0, block_rows - 1) * (col_count * depth_count)
        + receivers[0, :, 1] * depth_count
        + receivers[0, :, 2]
    )

    def inject_source(field, amount):
        return field.at[source_clip, source[0, 1], source[0, 2]].add(
            jnp.where(source_inside, amount, 0.0)
        )

    def inject_residual(field, values):
        flat_field = (
            field.reshape(-1).at[receiver_flat].add(jnp.where(receiver_inside, values, 0.0))
        )
        return flat_field.reshape(field.shape)

    previous = wave_before[0]
    current = wave_now[0]
    laplacians = []
    residuals = []
    for step_index in range(STEPS):
        forward_extended = with_halo(current, (("space", 0),), 4)
        laplace_now = stencil(side_pad(forward_extended), block_rows, col_count, depth_count)
        laplacians.append(laplace_now)
        next_field = inject_source(
            2.0 * current - previous + speed_window * laplace_now, wavelet[0, step_index]
        )
        residuals.append(
            jnp.where(receiver_inside, next_field.reshape(-1)[receiver_flat], 0.0)
            - observed[0, step_index]
        )
        previous, current = (current, next_field)
    farther = adjoint_after[0]
    nearer = inject_residual(adjoint_now[0], residuals[STEPS - 1])
    imaging = jnp.zeros((block_rows, col_count, depth_count), jnp.float32)
    following = current
    present = previous
    for step_index in range(STEPS - 1, -1, -1):
        if step_index > 0:
            paired = with_halo(jnp.stack([speed_window * nearer, present]), (("space", 1),), 4)
            adjoint_lap = stencil(side_pad(paired[0]), block_rows, col_count, depth_count)
            laplace_now = stencil(side_pad(paired[1]), block_rows, col_count, depth_count)
        else:
            extended = with_halo(present, (("space", 0),), 4)
            laplace_now = stencil(side_pad(extended), block_rows, col_count, depth_count)
        imaging = imaging + nearer * laplace_now
        if step_index > 0:
            updated = inject_residual(
                2.0 * nearer - farther + adjoint_lap, residuals[step_index - 1]
            )
            farther, nearer = (nearer, updated)
            earlier = inject_source(
                2.0 * present - following + speed_window * laplace_now, wavelet[0, step_index]
            )
            following, present = (present, earlier)
    spread_rows = jnp.zeros((block_rows, columns.shape[1], depth_count), jnp.float32)
    spread_rows = lax.dynamic_update_slice_in_dim(spread_rows, imaging, corner_y, 1)
    returned = lax.all_to_all(spread_rows, "space", split_axis=1, concat_axis=0, tiled=True)
    placed = lax.dynamic_update_slice_in_dim(
        jnp.zeros(all_rows.shape, jnp.float32), returned, corner_x, 0
    )
    return lax.psum_scatter(placed, "shot", scatter_dimension=0, tiled=True)


def solution(mesh):
    return jax.shard_map(
        on_device,
        mesh=mesh,
        in_specs=(
            P("shot", "space", None),
            P("shot", None),
            P("shot", None),
            P("shot", None),
            P("shot", None, None),
            P("shot", None, None),
            P("shot", "space", None, None),
            P("shot", "space", None, None),
            P("shot", "space", None, None),
            P("shot", "space", None, None),
        ),
        out_specs=P("shot", "space", None),
        check_vma=False,
    )
```

profile of v0, /device:TPU:64, one launch (start us, length us, event | category | flops | bytes accessed | tf_op | source)
XLA Modules:
  0.0 410.5 jit_solution(3708138599731003318)
XLA Ops:
  7.3 1.3 fusion.227
  10.5 89.0 %all-gather.2.cloned.1.call-done = f32[512,8,128]{2,1,0:T(8,128)} async-done(((f32[32,8,128]{2,1,0:T(8,128)}), f32[512,8,128]{2,1,0:T(8,128)}) %all-gather.2.cloned.1.call-update) | async-done | bytes 2097168 | tf_op jit(solution)/shard_map/all_gather | solution.py:68
  99.5 1.9 constant_dynamic-slice_fusion
  101.4 11.5 %all-to-all-start = ((f32[128,8,128]{2,1,0:T(8,128)}), f32[128,8,128]{2,1,0:T(8,128)S(1)}, u32[]{:S(2)}, u32[]{:S(2)}) async-start(f32[128,8,128]{2,1,0:T(8,128)} %constant_dynamic-slice_fusion), calls=%async_computation | async-start | bytes 1048576 | tf_op jit(solution)/shard_map/all_to_all | solution.py:70
  113.0 2.1 collective-permute-start.1
  115.1 8.3 %collective-permute-start = (f32[4,128,128]{2,1,0:T(8,128)S(1)}, f32[4,128,128]{2,1,0:T(8,128)S(1)}, u32[]{:S(2)}, u32[]{:S(2)}) collective-permute-start(f32[4,128,128]{2,1,0:T(8,128)S(1)} %bitcast.190), channel_id=1, source_target_pairs={{1,0},{2,1},{3,2},{4,3},{5,4},{6,5},{7,6},{8,7},{9,8},{10,9},{11,1... | collective-permute-start | bytes 786440 | tf_op jit(solution)/shard_map/ppermute | solution.py:20
  133.6 2.4 fusion.80
  138.4 4.0 collective-permute-start.3
  142.4 6.6 %collective-permute-start.2 = (f32[4,128,128]{2,1,0:T(8,128)S(1)}, f32[4,128,128]{2,1,0:T(8,128)S(1)}, u32[]{:S(2)}, u32[]{:S(2)}) collective-permute-start(f32[4,128,128]{2,1,0:T(8,128)S(1)} %scatter-add.36), channel_id=1, source_target_pairs={{1,0},{2,1},{3,2},{4,3},{5,4},{6,5},{7,6},{8,7},{9,8},{10,9},{11,1... | collective-permute-start | bytes 786440 | tf_op jit(solution)/shard_map/ppermute | solution.py:20
  150.3 3.2 collective-permute-done.3
  157.6 6.9 %collective-permute-start.5 = (f32[4,128,128]{2,1,0:T(8,128)S(1)}, f32[4,128,128]{2,1,0:T(8,128)S(1)}, u32[]{:S(2)}, u32[]{:S(2)}) collective-permute-start(f32[4,128,128]{2,1,0:T(8,128)S(1)} %scatter-add.39), channel_id=1, source_target_pairs={{0,1},{1,2},{2,3},{3,4},{4,5},{5,6},{6,7},{7,8},{8,9},{9,10},{10,1... | collective-permute-start | bytes 786440 | tf_op jit(solution)/shard_map/ppermute | solution.py:18
  164.5 3.4 collective-permute-start.4
  170.1 1.8 collective-permute-done.4
  178.0 6.2 %collective-permute-start.7 = (f32[2,4,128,128]{3,2,1,0:T(8,128)S(1)}, f32[2,4,128,128]{3,2,1,0:T(8,128)S(1)}, u32[]{:S(2)}, u32[]{:S(2)}) collective-permute-start(f32[2,4,128,128]{3,2,1,0:T(8,128)S(1)} %pad_maximum_fusion.4), channel_id=1, source_target_pairs={{0,1},{1,2},{2,3},{3,4},{4,5},{5,6},{6,7},{7,8},{8,9},{9,10},{10,1... | collective-permute-start | bytes 1572872 | tf_op jit(solution)/shard_map/ppermute | solution.py:18
  184.2 4.3 %collective-permute-start.6 = (f32[2,4,128,128]{3,2,1,0:T(8,128)S(1)}, f32[2,4,128,128]{3,2,1,0:T(8,128)S(1)}, u32[]{:S(2)}, u32[]{:S(2)}) collective-permute-start(f32[2,4,128,128]{3,2,1,0:T(8,128)S(1)} %pad_maximum_fusion.4), channel_id=1, source_target_pairs={{1,0},{2,1},{3,2},{4,3},{5,4},{6,5},{7,6},{8,7},{9,8},{10,9},{11,1... | collective-permute-start | bytes 1572872 | tf_op jit(solution)/shard_map/ppermute | solution.py:20
  188.5 4.9 %collective-permute-done.7 = f32[2,4,128,128]{3,2,1,0:T(8,128)S(1)} collective-permute-done((f32[2,4,128,128]{3,2,1,0:T(8,128)S(1)}, f32[2,4,128,128]{3,2,1,0:T(8,128)S(1)}, u32[]{:S(2)}, u32[]{:S(2)}) %collective-permute-start.7) | collective-permute-done | bytes 524320 | tf_op jit(solution)/shard_map/ppermute | solution.py:18
  193.4 6.0 %collective-permute-done.6 = f32[2,4,128,128]{3,2,1,0:T(8,128)S(1)} collective-permute-done((f32[2,4,128,128]{3,2,1,0:T(8,128)S(1)}, f32[2,4,128,128]{3,2,1,0:T(8,128)S(1)}, u32[]{:S(2)}, u32[]{:S(2)}) %collective-permute-start.6) | collective-permute-done | bytes 524320 | tf_op jit(solution)/shard_map/ppermute | solution.py:20
  203.2 5.7 %multiply_add_fusion.1 = (f32[4,128,128]{2,1,0:T(8,128)S(1)}, f32[4,128,128]{2,1,0:T(8,128)}, f32[1,4,128,128]{3,2,1,0:T(8,128)}) fusion(f32[4,128,128]{2,1,0:T(8,128)S(1)} %scatter-add.48, f32[4,128,128]{2,1,0:T(8,128)S(1)} %scatter-add.39, f32[4,256,128]{2,1,0:T(8,128)S(1)} %bitcast.170, s32[]{:T(128)S(6)} %select_n.75, ...), kind=kLoop, calls=%fused_computation.405 | loop fusion | flops 2228224 | bytes 4718596 | tf_op jit(solution)/shard_map/add | solution.py:130
  212.5 5.6 %collective-permute-start.9 = (f32[2,4,128,128]{3,2,1,0:T(8,128)S(1)}, f32[2,4,128,128]{3,2,1,0:T(8,128)S(1)}, u32[]{:S(2)}, u32[]{:S(2)}) collective-permute-start(f32[2,4,128,128]{3,2,1,0:T(8,128)S(1)} %pad_maximum_fusion.5), channel_id=1, source_target_pairs={{0,1},{1,2},{2,3},{3,4},{4,5},{5,6},{6,7},{7,8},{8,9},{9,10},{10,1... | collective-permute-start | bytes 1572872 | tf_op jit(solution)/shard_map/ppermute | solution.py:18
  218.1 5.1 %collective-permute-start.8 = (f32[2,4,128,128]{3,2,1,0:T(8,128)S(1)}, f32[2,4,128,128]{3,2,1,0:T(8,128)S(1)}, u32[]{:S(2)}, u32[]{:S(2)}) collective-permute-start(f32[2,4,128,128]{3,2,1,0:T(8,128)S(1)} %pad_maximum_fusion.5), channel_id=1, source_target_pairs={{1,0},{2,1},{3,2},{4,3},{5,4},{6,5},{7,6},{8,7},{9,8},{10,9},{11,1... | collective-permute-start | bytes 1572872 | tf_op jit(solution)/shard_map/ppermute | solution.py:20
  223.2 4.8 %collective-permute-done.9 = f32[2,4,128,128]{3,2,1,0:T(8,128)S(1)} collective-permute-done((f32[2,4,128,128]{3,2,1,0:T(8,128)S(1)}, f32[2,4,128,128]{3,2,1,0:T(8,128)S(1)}, u32[]{:S(2)}, u32[]{:S(2)}) %collective-permute-start.9) | collective-permute-done | bytes 524320 | tf_op jit(solution)/shard_map/ppermute | solution.py:18
  228.0 3.0 collective-permute-done.8
  231.1 1.2 pad_maximum_fusion.1
  233.5 1.3 multiply_add_fusion
  237.7 7.0 %collective-permute-start.11 = (f32[4,128,128]{2,1,0:T(8,128)S(1)}, f32[4,128,128]{2,1,0:T(8,128)}, u32[]{:S(2)}, u32[]{:S(2)}) collective-permute-start(f32[4,128,128]{2,1,0:T(8,128)S(1)} %scatter-add.53), channel_id=1, source_target_pairs={{0,1},{1,2},{2,3},{3,4},{4,5},{5,6},{6,7},{7,8},{8,9},{9,10},{10,1... | collective-permute-start | bytes 786440 | tf_op jit(solution)/shard_map/ppermute | solution.py:18
  244.7 3.7 collective-permute-start.10
  248.4 5.1 %fusion.173 = f32[4,128,128]{2,1,0:T(8,128)S(1)} fusion(f32[12,128,128]{2,1,0:T(8,128)} %get-tuple-element.70, f32[2,4,128,128]{3,2,1,0:T(8,128)S(1)} %collective-permute-done.9, f32[2,4,128,128]{3,2,1,0:T(8,128)} %copy-done.4, f32[2,8,128,128]{3,2,1,0:T(8,128)} %copy-done.2, f32[2,8,128,128]{3,2,1,0:T(8,128)S(1)} %get-tuple-element.73, ...), kind=kLoop, calls=%fused_computation.301 | loop fusion | flops 2162688 | bytes 3932164 | tf_op jit(solution)/shard_map/add | solution.py:126
  254.6 1.5 select_maximum_fusion
  256.1 2.4 fusion.14
  258.9 45.0 %all_to_all.36 = f32[4,256,128]{2,0,1:T(4,128)S(1)} all-to-all(f32[4,256,128]{2,0,1:T(4,128)S(1)} %copy_dynamic-update-slice_fusion), channel_id=1, replica_groups=mesh['shot'=16,'space'=32] {'space'}, dimensions={1} | all-to-all | bytes 1048576 | tf_op jit(solution)/shard_map/all_to_all | solution.py:135
  304.2 1.4 copy-done.1
  305.6 98.0 %reduce-scatter.2.cloned.1.call-done = f32[32,8,128]{2,1,0:T(8,128)} async-done(((f32[512,8,128]{2,1,0:T(8,128)}), f32[32,8,128]{2,1,0:T(8,128)}) %reduce-scatter.2.cloned.1.call-update) | async-done | bytes 131088 | tf_op jit(solution)/shard_map/reduce_scatter | solution.py:139
  (87 shorter events, 22.4 us)
Async XLA Ops:
  6.5 125.1 %copy-start.16 = (s32[3]{0:T(128)S(1)}, s32[3]{0:T(128)}, u32[]{:S(2)}) copy-start(s32[3]{0:T(128)} %constant.131.clone.1) | copy-start | bytes 40
  6.5 116.9 %copy-start.12 = (s32[1,3]{1,0:T(1,128)S(1)}, s32[1,3]{1,0:T(1,128)}, u32[]{:S(2)}) copy-start(s32[1,3]{1,0:T(1,128)} %param.22) | copy-start | bytes 40
  6.5 123.9 %copy-start.13 = (f32[1,3]{1,0:T(1,128)S(1)}, f32[1,3]{1,0:T(1,128)}, u32[]{:S(2)}) copy-start(f32[1,3]{1,0:T(1,128)} %param.23) | copy-start | bytes 40
  6.5 106.5 %copy-start.7 = (f32[1,4,128,128]{3,2,1,0:T(8,128)S(1)}, f32[1,4,128,128]{3,2,1,0:T(8,128)}, u32[]{:S(2)}) copy-start(f32[1,4,128,128]{3,2,1,0:T(8,128)} %param.27) | copy-start | bytes 786436
  6.5 93.0 %all-gather.2.cloned.1.call-start = ((), (), s32[]{:S(2)}) async-start(), calls=%async_computation.3 | async-start | bytes 2228224 | tf_op jit(solution)/shard_map/all_gather | solution.py:68
  101.4 31.9 %all-to-all-start = ((f32[128,8,128]{2,1,0:T(8,128)}), f32[128,8,128]{2,1,0:T(8,128)S(1)}, u32[]{:S(2)}, u32[]{:S(2)}) async-start(f32[128,8,128]{2,1,0:T(8,128)} %constant_dynamic-slice_fusion), calls=%async_computation | async-start | bytes 1048576 | tf_op jit(solution)/shard_map/all_to_all | solution.py:70
  113.0 290.6 %reduce-scatter.2.cloned.1.call-start = ((), (), s32[]{:S(2)}) async-start(), calls=%async_computation.4 | async-start | bytes 2228224 | tf_op jit(solution)/shard_map/reduce_scatter | solution.py:139
  113.0 19.4 %collective-permute-start.1 = (f32[4,128,128]{2,1,0:T(8,128)S(1)}, f32[4,128,128]{2,1,0:T(8,128)S(1)}, u32[]{:S(2)}, u32[]{:S(2)}) collective-permute-start(f32[4,128,128]{2,1,0:T(8,128)S(1)} %bitcast.189), channel_id=1, source_target_pairs={{0,1},{1,2},{2,3},{3,4},{4,5},{5,6},{6,7},{7,8},{8,9},{9,10},{10,1... | collective-permute-start | bytes 786440 | tf_op jit(solution)/shard_map/ppermute | solution.py:18
  115.1 17.7 %collective-permute-start = (f32[4,128,128]{2,1,0:T(8,128)S(1)}, f32[4,128,128]{2,1,0:T(8,128)S(1)}, u32[]{:S(2)}, u32[]{:S(2)}) collective-permute-start(f32[4,128,128]{2,1,0:T(8,128)S(1)} %bitcast.190), channel_id=1, source_target_pairs={{1,0},{2,1},{3,2},{4,3},{5,4},{6,5},{7,6},{8,7},{9,8},{10,9},{11,1... | collective-permute-start | bytes 786440 | tf_op jit(solution)/shard_map/ppermute | solution.py:20
  132.8 0.7 copy-start.9
  138.4 15.1 %collective-permute-start.3 = (f32[4,128,128]{2,1,0:T(8,128)S(1)}, f32[4,128,128]{2,1,0:T(8,128)S(1)}, u32[]{:S(2)}, u32[]{:S(2)}) collective-permute-start(f32[4,128,128]{2,1,0:T(8,128)S(1)} %scatter-add.36), channel_id=1, source_target_pairs={{0,1},{1,2},{2,3},{3,4},{4,5},{5,6},{6,7},{7,8},{8,9},{9,10},{10,1... | collective-permute-start | bytes 786440 | tf_op jit(solution)/shard_map/ppermute | solution.py:18
  142.4 11.1 %collective-permute-start.2 = (f32[4,128,128]{2,1,0:T(8,128)S(1)}, f32[4,128,128]{2,1,0:T(8,128)S(1)}, u32[]{:S(2)}, u32[]{:S(2)}) collective-permute-start(f32[4,128,128]{2,1,0:T(8,128)S(1)} %scatter-add.36), channel_id=1, source_target_pairs={{1,0},{2,1},{3,2},{4,3},{5,4},{6,5},{7,6},{8,7},{9,8},{10,9},{11,1... | collective-permute-start | bytes 786440 | tf_op jit(solution)/shard_map/ppermute | solution.py:20
  154.0 14.0 %copy-start.14 = (s32[1,64,3]{1,0,2:T(1,128)S(1)}, s32[1,64,3]{1,0,2:T(1,128)}, u32[]{:S(2)}) copy-start(s32[1,64,3]{1,0,2:T(1,128)} %param.24) | copy-start | bytes 2308
  157.6 12.5 %collective-permute-start.5 = (f32[4,128,128]{2,1,0:T(8,128)S(1)}, f32[4,128,128]{2,1,0:T(8,128)S(1)}, u32[]{:S(2)}, u32[]{:S(2)}) collective-permute-start(f32[4,128,128]{2,1,0:T(8,128)S(1)} %scatter-add.39), channel_id=1, source_target_pairs={{0,1},{1,2},{2,3},{3,4},{4,5},{5,6},{6,7},{7,8},{8,9},{9,10},{10,1... | collective-permute-start | bytes 786440 | tf_op jit(solution)/shard_map/ppermute | solution.py:18
  164.5 7.3 %collective-permute-start.4 = (f32[4,128,128]{2,1,0:T(8,128)S(1)}, f32[4,128,128]{2,1,0:T(8,128)S(1)}, u32[]{:S(2)}, u32[]{:S(2)}) collective-permute-start(f32[4,128,128]{2,1,0:T(8,128)S(1)} %scatter-add.39), channel_id=1, source_target_pairs={{1,0},{2,1},{3,2},{4,3},{5,4},{6,5},{7,6},{8,7},{9,8},{10,9},{11,1... | collective-permute-start | bytes 786440 | tf_op jit(solution)/shard_map/ppermute | solution.py:20
  172.4 4.4 %copy-start.15 = (f32[1,3,64]{2,0,1:T(1,128)S(1)}, f32[1,3,64]{2,0,1:T(1,128)}, u32[]{:S(2)}) copy-start(f32[1,3,64]{2,0,1:T(1,128)} %param.25) | copy-start | bytes 2308
  172.4 4.4 %copy-start = (f32[1,4,128,128]{3,2,1,0:T(8,128)S(1)}, f32[1,4,128,128]{3,2,1,0:T(8,128)}, u32[]{:S(2)}) copy-start(f32[1,4,128,128]{3,2,1,0:T(8,128)} %param.29) | copy-start | bytes 786436
  178.0 15.5 %collective-permute-start.7 = (f32[2,4,128,128]{3,2,1,0:T(8,128)S(1)}, f32[2,4,128,128]{3,2,1,0:T(8,128)S(1)}, u32[]{:S(2)}, u32[]{:S(2)}) collective-permute-start(f32[2,4,128,128]{3,2,1,0:T(8,128)S(1)} %pad_maximum_fusion.4), channel_id=1, source_target_pairs={{0,1},{1,2},{2,3},{3,4},{4,5},{5,6},{6,7},{7,8},{8,9},{9,10},{10,1... | collective-permute-start | bytes 1572872 | tf_op jit(solution)/shard_map/ppermute | solution.py:18
  184.2 15.3 %collective-permute-start.6 = (f32[2,4,128,128]{3,2,1,0:T(8,128)S(1)}, f32[2,4,128,128]{3,2,1,0:T(8,128)S(1)}, u32[]{:S(2)}, u32[]{:S(2)}) collective-permute-start(f32[2,4,128,128]{3,2,1,0:T(8,128)S(1)} %pad_maximum_fusion.4), channel_id=1, source_target_pairs={{1,0},{2,1},{3,2},{4,3},{5,4},{6,5},{7,6},{8,7},{9,8},{10,9},{11,1... | collective-permute-start | bytes 1572872 | tf_op jit(solution)/shard_map/ppermute | solution.py:20
  199.5 1.3 copy-start.5
  200.6 0.9 copy-start.11
  200.8 1.4 copy-start.3
  212.5 15.6 %collective-permute-start.9 = (f32[2,4,128,128]{3,2,1,0:T(8,128)S(1)}, f32[2,4,128,128]{3,2,1,0:T(8,128)S(1)}, u32[]{:S(2)}, u32[]{:S(2)}) collective-permute-start(f32[2,4,128,128]{3,2,1,0:T(8,128)S(1)} %pad_maximum_fusion.5), channel_id=1, source_target_pairs={{0,1},{1,2},{2,3},{3,4},{4,5},{5,6},{6,7},{7,8},{8,9},{9,10},{10,1... | collective-permute-start | bytes 1572872 | tf_op jit(solution)/shard_map/ppermute | solution.py:18
  218.1 13.0 %collective-permute-start.8 = (f32[2,4,128,128]{3,2,1,0:T(8,128)S(1)}, f32[2,4,128,128]{3,2,1,0:T(8,128)S(1)}, u32[]{:S(2)}, u32[]{:S(2)}) collective-permute-start(f32[2,4,128,128]{3,2,1,0:T(8,128)S(1)} %pad_maximum_fusion.5), channel_id=1, source_target_pairs={{1,0},{2,1},{3,2},{4,3},{5,4},{6,5},{7,6},{8,7},{9,8},{10,9},{11,1... | collective-permute-start | bytes 1572872 | tf_op jit(solution)/shard_map/ppermute | solution.py:20
  231.1 2.4 copy-start.4
  232.3 1.0 copy-start.6
  233.5 1.4 copy-start.2
  237.7 16.8 %collective-permute-start.11 = (f32[4,128,128]{2,1,0:T(8,128)S(1)}, f32[4,128,128]{2,1,0:T(8,128)}, u32[]{:S(2)}, u32[]{:S(2)}) collective-permute-start(f32[4,128,128]{2,1,0:T(8,128)S(1)} %scatter-add.53), channel_id=1, source_target_pairs={{0,1},{1,2},{2,3},{3,4},{4,5},{5,6},{6,7},{7,8},{8,9},{9,10},{10,1... | collective-permute-start | bytes 786440 | tf_op jit(solution)/shard_map/ppermute | solution.py:18
  244.7 9.9 %collective-permute-start.10 = (f32[4,128,128]{2,1,0:T(8,128)S(1)}, f32[4,128,128]{2,1,0:T(8,128)}, u32[]{:S(2)}, u32[]{:S(2)}) collective-permute-start(f32[4,128,128]{2,1,0:T(8,128)S(1)} %scatter-add.53), channel_id=1, source_target_pairs={{1,0},{2,1},{3,2},{4,3},{5,4},{6,5},{7,6},{8,7},{9,8},{10,9},{11,1... | collective-permute-start | bytes 786440 | tf_op jit(solution)/shard_map/ppermute | solution.py:20
  253.5 2.6 copy-start.8
  253.5 2.6 copy-start.10
  304.2 1.4 copy-start.1
Sparse Core Ops, SparseCore 0:
  9.5 90.0 all-gather.1
  305.7 97.8 reduce-scatter.1
where the time goes:
time: 411 us; the launch traced here: 410 us
  waiting for transfers between devices  212 us (52%)
  starting transfers between devices  74.8 us (18%)
  blocking collectives  45 us (11%)
  between operations  33.1 us (8%)
  other arithmetic  29.6 us (7%)
  local copies, waits for them, and re-layouts  15.4 us (4%)
    reduce_scatter x1, waiting for transfers between devices, on_device(): return lax.psum_scatter(placed, 'shot', scatter_dimension=0, tiled=True)  98 us
    all_gather x1, waiting for transfers between devices, on_device(): all_rows = lax.all_gather(courant, 'shot', axis=0, tiled=True)  89 us
    all_to_all x1, blocking collectives, on_device(): lax.all_to_all(spread_rows, 'space', split_axis=1, concat_axis=0, tiled=T...  45 us
    ppermute x6, starting transfers between devices, with_halo(): lax.ppermute(tail, axis, [(i, (i + 1) % count) for i in range(ends)])  31.7 us
    ppermute x6, starting transfers between devices, with_halo(): lax.ppermute(head, axis, [((i + 1) % count, i) for i in range(ends)])  31.5 us
    ppermute x6, waiting for transfers between devices, with_halo(): lax.ppermute(tail, axis, [(i, (i + 1) % count) for i in range(ends)])  13.5 us
    all_to_all x1, starting transfers between devices, on_device(): lax.all_to_all(window, 'space', split_axis=0, concat_axis=1, tiled=True)  11.5 us
    ppermute x6, waiting for transfers between devices, with_halo(): lax.ppermute(head, axis, [((i + 1) % count, i) for i in range(ends)])  11.2 us
  transfers between devices with their start and end apart: 15, of which 10 were waited for; matrix products, arithmetic and copies ran while one was open for 3% of the time, Pallas kernels for 0%

commit v1 on v0

--- a/solution.py
+++ b/solution.py
@@ -67,7 +67,10 @@
     corner_y = anchor[0, 1]
     all_rows = lax.all_gather(courant, "shot", axis=0, tiled=True)
     window = lax.dynamic_slice_in_dim(all_rows, corner_x, block_rows * space_count, 0)
-    columns = lax.all_to_all(window, "space", split_axis=0, concat_axis=1, tiled=True)
+    columns = jnp.concatenate(
+        lax.all_to_all(jnp.stack(jnp.split(window, lax.axis_size("space"), axis=0)), "space", 0, 0),
+        axis=1,
+    )
     speed_window = lax.dynamic_slice_in_dim(columns, corner_y, col_count, 1)
     source_row = source[0, 0] - start_row
     source_inside = (source_row >= 0) & (source_row < block_rows)

time: 411 us -> 454 us (1.10)
  local copies, waits for them, and re-layouts: 15.4 us -> 55.7 us
    unnamed x34 -> x65, local copies, waits for them, and re-layouts: 2.33 us -> 43.1 us
where the time goes in v1:
time: 454 us; the launch traced here: 450 us
  waiting for transfers between devices  212 us (47%)
  starting transfers between devices  74.8 us (16%)
  local copies, waits for them, and re-layouts  55.7 us (12%)
  blocking collectives  45 us (10%)
  between operations  33.2 us (7%)
  other arithmetic  29.6 us (7%)
    reduce_scatter x1, waiting for transfers between devices, on_device(): return lax.psum_scatter(placed, 'shot', scatter_dimension=0, tiled=True)  97.7 us
    all_gather x1, waiting for transfers between devices, on_device(): all_rows = lax.all_gather(courant, 'shot', axis=0, tiled=True)  89 us
    all_to_all x1, blocking collectives, on_device(): lax.all_to_all(spread_rows, 'space', split_axis=1, concat_axis=0, tiled=T...  45 us
    unnamed x65, local copies, waits for them, and re-layouts  43.1 us
    ppermute x6, starting transfers between devices, with_halo(): lax.ppermute(tail, axis, [(i, (i + 1) % count) for i in range(ends)])  31.7 us
    ppermute x6, starting transfers between devices, with_halo(): lax.ppermute(head, axis, [((i + 1) % count, i) for i in range(ends)])  31.5 us
    ppermute x6, waiting for transfers between devices, with_halo(): lax.ppermute(tail, axis, [(i, (i + 1) % count) for i in range(ends)])  13.5 us
    all_to_all x1, starting transfers between devices, on_device(): lax.all_to_all(jnp.stack(jnp.split(window, lax.axis_size('space'), axis=0...  11.5 us
  transfers between devices with their start and end apart: 15, of which 10 were waited for; matrix products, arithmetic and copies ran while one was open for 3% of the time, Pallas kernels for 0%

profile of v1, /device:TPU:64, one launch (start us, length us, event | category | flops | bytes accessed | tf_op | source)
XLA Modules:
  0.0 450.4 jit_solution(6225607936541752890)
XLA Ops:
  7.3 1.3 fusion.227
  10.5 89.0 %all-gather.2.cloned.1.call-done = f32[512,8,128]{2,1,0:T(8,128)} async-done(((f32[32,8,128]{2,1,0:T(8,128)}), f32[512,8,128]{2,1,0:T(8,128)}) %all-gather.2.cloned.1.call-update) | async-done | bytes 2097168 | tf_op jit(solution)/shard_map/all_gather | solution.py:68
  106.1 1.3 constant_dynamic-update-slice_fusion.26
  133.8 1.3 constant_dynamic-update-slice_fusion.5
  141.7 11.5 %all-to-all-start = ((f32[32,4,8,128]{3,2,1,0:T(8,128)}), f32[32,4,8,128]{3,2,1,0:T(8,128)S(1)}, u32[]{:S(2)}, u32[]{:S(2)}) async-start(f32[32,4,8,128]{3,2,1,0:T(8,128)} %constant_dynamic-update-slice_fusion), calls=%async_computation | async-start | bytes 1048576 | tf_op jit(solution)/shard_map/all_to_all | solution.py:71
  153.3 2.1 collective-permute-start.1
  155.3 8.3 %collective-permute-start = (f32[4,128,128]{2,1,0:T(8,128)S(1)}, f32[4,128,128]{2,1,0:T(8,128)S(1)}, u32[]{:S(2)}, u32[]{:S(2)}) collective-permute-start(f32[4,128,128]{2,1,0:T(8,128)S(1)} %bitcast.317), channel_id=1, source_target_pairs={{1,0},{2,1},{3,2},{4,3},{5,4},{6,5},{7,6},{8,7},{9,8},{10,9},{11,1... | collective-permute-start | bytes 786440 | tf_op jit(solution)/shard_map/ppermute | solution.py:20
  173.8 2.4 fusion.80
  178.7 4.0 collective-permute-start.3
  182.6 6.6 %collective-permute-start.2 = (f32[4,128,128]{2,1,0:T(8,128)S(1)}, f32[4,128,128]{2,1,0:T(8,128)S(1)}, u32[]{:S(2)}, u32[]{:S(2)}) collective-permute-start(f32[4,128,128]{2,1,0:T(8,128)S(1)} %scatter-add.36), channel_id=1, source_target_pairs={{1,0},{2,1},{3,2},{4,3},{5,4},{6,5},{7,6},{8,7},{9,8},{10,9},{11,1... | collective-permute-start | bytes 786440 | tf_op jit(solution)/shard_map/ppermute | solution.py:20
  190.6 3.2 collective-permute-done.3
  197.9 6.9 %collective-permute-start.5 = (f32[4,128,128]{2,1,0:T(8,128)S(1)}, f32[4,128,128]{2,1,0:T(8,128)S(1)}, u32[]{:S(2)}, u32[]{:S(2)}) collective-permute-start(f32[4,128,128]{2,1,0:T(8,128)S(1)} %scatter-add.39), channel_id=1, source_target_pairs={{0,1},{1,2},{2,3},{3,4},{4,5},{5,6},{6,7},{7,8},{8,9},{9,10},{10,1... | collective-permute-start | bytes 786440 | tf_op jit(solution)/shard_map/ppermute | solution.py:18
  204.8 3.4 collective-permute-start.4
  210.4 1.8 collective-permute-done.4
  218.2 6.2 %collective-permute-start.7 = (f32[2,4,128,128]{3,2,1,0:T(8,128)S(1)}, f32[2,4,128,128]{3,2,1,0:T(8,128)S(1)}, u32[]{:S(2)}, u32[]{:S(2)}) collective-permute-start(f32[2,4,128,128]{3,2,1,0:T(8,128)S(1)} %pad_maximum_fusion.4), channel_id=1, source_target_pairs={{0,1},{1,2},{2,3},{3,4},{4,5},{5,6},{6,7},{7,8},{8,9},{9,10},{10,1... | collective-permute-start | bytes 1572872 | tf_op jit(solution)/shard_map/ppermute | solution.py:18
  224.4 4.3 collective-permute-start.6
  228.8 4.9 %collective-permute-done.7 = f32[2,4,128,128]{3,2,1,0:T(8,128)S(1)} collective-permute-done((f32[2,4,128,128]{3,2,1,0:T(8,128)S(1)}, f32[2,4,128,128]{3,2,1,0:T(8,128)S(1)}, u32[]{:S(2)}, u32[]{:S(2)}) %collective-permute-start.7) | collective-permute-done | bytes 524320 | tf_op jit(solution)/shard_map/ppermute | solution.py:18
  233.7 6.0 %collective-permute-done.6 = f32[2,4,128,128]{3,2,1,0:T(8,128)S(1)} collective-permute-done((f32[2,4,128,128]{3,2,1,0:T(8,128)S(1)}, f32[2,4,128,128]{3,2,1,0:T(8,128)S(1)}, u32[]{:S(2)}, u32[]{:S(2)}) %collective-permute-start.6) | collective-permute-done | bytes 524320 | tf_op jit(solution)/shard_map/ppermute | solution.py:20
  243.5 5.7 %multiply_add_fusion.1 = (f32[4,128,128]{2,1,0:T(8,128)S(1)}, f32[4,128,128]{2,1,0:T(8,128)}, f32[1,4,128,128]{3,2,1,0:T(8,128)}) fusion(f32[4,128,128]{2,1,0:T(8,128)S(1)} %scatter-add.48, f32[4,128,128]{2,1,0:T(8,128)S(1)} %scatter-add.39, f32[4,256,128]{2,1,0:T(8,128)S(1)} %bitcast.297, s32[]{:T(128)S(6)} %select_n.75, ...), kind=kLoop, calls=%fused_computation.405 | loop fusion | flops 2228224 | bytes 4718596 | tf_op jit(solution)/shard_map/add | solution.py:133
  252.7 5.6 %collective-permute-start.9 = (f32[2,4,128,128]{3,2,1,0:T(8,128)S(1)}, f32[2,4,128,128]{3,2,1,0:T(8,128)S(1)}, u32[]{:S(2)}, u32[]{:S(2)}) collective-permute-start(f32[2,4,128,128]{3,2,1,0:T(8,128)S(1)} %pad_maximum_fusion.5), channel_id=1, source_target_pairs={{0,1},{1,2},{2,3},{3,4},{4,5},{5,6},{6,7},{7,8},{8,9},{9,10},{10,1... | collective-permute-start | bytes 1572872 | tf_op jit(solution)/shard_map/ppermute | solution.py:18
  258.3 5.1 %collective-permute-start.8 = (f32[2,4,128,128]{3,2,1,0:T(8,128)S(1)}, f32[2,4,128,128]{3,2,1,0:T(8,128)S(1)}, u32[]{:S(2)}, u32[]{:S(2)}) collective-permute-start(f32[2,4,128,128]{3,2,1,0:T(8,128)S(1)} %pad_maximum_fusion.5), channel_id=1, source_target_pairs={{1,0},{2,1},{3,2},{4,3},{5,4},{6,5},{7,6},{8,7},{9,8},{10,9},{11,1... | collective-permute-start | bytes 1572872 | tf_op jit(solution)/shard_map/ppermute | solution.py:20
  263.5 4.8 %collective-permute-done.9 = f32[2,4,128,128]{3,2,1,0:T(8,128)S(1)} collective-permute-done((f32[2,4,128,128]{3,2,1,0:T(8,128)S(1)}, f32[2,4,128,128]{3,2,1,0:T(8,128)S(1)}, u32[]{:S(2)}, u32[]{:S(2)}) %collective-permute-start.9) | collective-permute-done | bytes 524320 | tf_op jit(solution)/shard_map/ppermute | solution.py:18
  268.3 3.0 collective-permute-done.8
  273.8 1.3 multiply_add_fusion
  278.0 7.0 %collective-permute-start.11 = (f32[4,128,128]{2,1,0:T(8,128)S(1)}, f32[4,128,128]{2,1,0:T(8,128)}, u32[]{:S(2)}, u32[]{:S(2)}) collective-permute-start(f32[4,128,128]{2,1,0:T(8,128)S(1)} %scatter-add.53), channel_id=1, source_target_pairs={{0,1},{1,2},{2,3},{3,4},{4,5},{5,6},{6,7},{7,8},{8,9},{9,10},{10,1... | collective-permute-start | bytes 786440 | tf_op jit(solution)/shard_map/ppermute | solution.py:18
  284.9 3.7 collective-permute-start.10
  288.6 5.1 %fusion.173 = f32[4,128,128]{2,1,0:T(8,128)S(1)} fusion(f32[12,128,128]{2,1,0:T(8,128)} %get-tuple-element.70, f32[2,4,128,128]{3,2,1,0:T(8,128)S(1)} %collective-permute-done.9, f32[2,4,128,128]{3,2,1,0:T(8,128)} %copy-done.4, f32[2,8,128,128]{3,2,1,0:T(8,128)} %copy-done.2, f32[2,8,128,128]{3,2,1,0:T(8,128)S(1)} %get-tuple-element.73, ...), kind=kLoop, calls=%fused_computation.301 | loop fusion | flops 2162688 | bytes 3932164 | tf_op jit(solution)/shard_map/add | solution.py:129
  294.8 1.5 select_maximum_fusion
  296.4 2.4 fusion.14
  299.1 45.0 %all_to_all.23 = f32[4,256,128]{2,0,1:T(4,128)S(1)} all-to-all(f32[4,256,128]{2,0,1:T(4,128)S(1)} %copy_dynamic-update-slice_fusion), channel_id=1, replica_groups=mesh['shot'=16,'space'=32] {'space'}, dimensions={1} | all-to-all | bytes 1048576 | tf_op jit(solution)/shard_map/all_to_all | solution.py:138
  344.5 1.4 copy-done.1
  345.9 97.7 %reduce-scatter.2.cloned.1.call-done = f32[32,8,128]{2,1,0:T(8,128)} async-done(((f32[512,8,128]{2,1,0:T(8,128)}), f32[32,8,128]{2,1,0:T(8,128)}) %reduce-scatter.2.cloned.1.call-update) | async-done | bytes 131088 | tf_op jit(solution)/shard_map/reduce_scatter | solution.py:142
  (118 shorter events, 63.1 us)
Async XLA Ops:
  6.5 165.4 %copy-start.16 = (s32[3]{0:T(128)S(1)}, s32[3]{0:T(128)}, u32[]{:S(2)}) copy-start(s32[3]{0:T(128)} %constant.131.clone.1) | copy-start | bytes 40
  6.5 157.1 %copy-start.12 = (s32[1,3]{1,0:T(1,128)S(1)}, s32[1,3]{1,0:T(1,128)}, u32[]{:S(2)}) copy-start(s32[1,3]{1,0:T(1,128)} %param.22) | copy-start | bytes 40
  6.5 164.1 %copy-start.13 = (f32[1,3]{1,0:T(1,128)S(1)}, f32[1,3]{1,0:T(1,128)}, u32[]{:S(2)}) copy-start(f32[1,3]{1,0:T(1,128)} %param.23) | copy-start | bytes 40
  6.5 146.7 %copy-start.7 = (f32[1,4,128,128]{3,2,1,0:T(8,128)S(1)}, f32[1,4,128,128]{3,2,1,0:T(8,128)}, u32[]{:S(2)}) copy-start(f32[1,4,128,128]{3,2,1,0:T(8,128)} %param.27) | copy-start | bytes 786436
  6.5 93.0 %all-gather.2.cloned.1.call-start = ((), (), s32[]{:S(2)}) async-start(), calls=%async_computation.3 | async-start | bytes 2228224 | tf_op jit(solution)/shard_map/all_gather | solution.py:68
  141.7 32.1 %all-to-all-start = ((f32[32,4,8,128]{3,2,1,0:T(8,128)}), f32[32,4,8,128]{3,2,1,0:T(8,128)S(1)}, u32[]{:S(2)}, u32[]{:S(2)}) async-start(f32[32,4,8,128]{3,2,1,0:T(8,128)} %constant_dynamic-update-slice_fusion), calls=%async_computation | async-start | bytes 1048576 | tf_op jit(solution)/shard_map/all_to_all | solution.py:71
  153.2 290.3 %reduce-scatter.2.cloned.1.call-start = ((), (), s32[]{:S(2)}) async-start(), calls=%async_computation.4 | async-start | bytes 2228224 | tf_op jit(solution)/shard_map/reduce_scatter | solution.py:142
  153.3 19.4 %collective-permute-start.1 = (f32[4,128,128]{2,1,0:T(8,128)S(1)}, f32[4,128,128]{2,1,0:T(8,128)S(1)}, u32[]{:S(2)}, u32[]{:S(2)}) collective-permute-start(f32[4,128,128]{2,1,0:T(8,128)S(1)} %bitcast.316), channel_id=1, source_target_pairs={{0,1},{1,2},{2,3},{3,4},{4,5},{5,6},{6,7},{7,8},{8,9},{9,10},{10,1... | collective-permute-start | bytes 786440 | tf_op jit(solution)/shard_map/ppermute | solution.py:18
  155.3 17.7 %collective-permute-start = (f32[4,128,128]{2,1,0:T(8,128)S(1)}, f32[4,128,128]{2,1,0:T(8,128)S(1)}, u32[]{:S(2)}, u32[]{:S(2)}) collective-permute-start(f32[4,128,128]{2,1,0:T(8,128)S(1)} %bitcast.317), channel_id=1, source_target_pairs={{1,0},{2,1},{3,2},{4,3},{5,4},{6,5},{7,6},{8,7},{9,8},{10,9},{11,1... | collective-permute-start | bytes 786440 | tf_op jit(solution)/shard_map/ppermute | solution.py:20
  173.1 0.7 copy-start.9
  178.7 15.1 %collective-permute-start.3 = (f32[4,128,128]{2,1,0:T(8,128)S(1)}, f32[4,128,128]{2,1,0:T(8,128)S(1)}, u32[]{:S(2)}, u32[]{:S(2)}) collective-permute-start(f32[4,128,128]{2,1,0:T(8,128)S(1)} %scatter-add.36), channel_id=1, source_target_pairs={{0,1},{1,2},{2,3},{3,4},{4,5},{5,6},{6,7},{7,8},{8,9},{9,10},{10,1... | collective-permute-start | bytes 786440 | tf_op jit(solution)/shard_map/ppermute | solution.py:18
  182.6 11.1 %collective-permute-start.2 = (f32[4,128,128]{2,1,0:T(8,128)S(1)}, f32[4,128,128]{2,1,0:T(8,128)S(1)}, u32[]{:S(2)}, u32[]{:S(2)}) collective-permute-start(f32[4,128,128]{2,1,0:T(8,128)S(1)} %scatter-add.36), channel_id=1, source_target_pairs={{1,0},{2,1},{3,2},{4,3},{5,4},{6,5},{7,6},{8,7},{9,8},{10,9},{11,1... | collective-permute-start | bytes 786440 | tf_op jit(solution)/shard_map/ppermute | solution.py:20
  194.3 14.0 %copy-start.14 = (s32[1,64,3]{1,0,2:T(1,128)S(1)}, s32[1,64,3]{1,0,2:T(1,128)}, u32[]{:S(2)}) copy-start(s32[1,64,3]{1,0,2:T(1,128)} %param.24) | copy-start | bytes 2308
  197.9 12.5 %collective-permute-start.5 = (f32[4,128,128]{2,1,0:T(8,128)S(1)}, f32[4,128,128]{2,1,0:T(8,128)S(1)}, u32[]{:S(2)}, u32[]{:S(2)}) collective-permute-start(f32[4,128,128]{2,1,0:T(8,128)S(1)} %scatter-add.39), channel_id=1, source_target_pairs={{0,1},{1,2},{2,3},{3,4},{4,5},{5,6},{6,7},{7,8},{8,9},{9,10},{10,1... | collective-permute-start | bytes 786440 | tf_op jit(solution)/shard_map/ppermute | solution.py:18
  204.8 7.3 %collective-permute-start.4 = (f32[4,128,128]{2,1,0:T(8,128)S(1)}, f32[4,128,128]{2,1,0:T(8,128)S(1)}, u32[]{:S(2)}, u32[]{:S(2)}) collective-permute-start(f32[4,128,128]{2,1,0:T(8,128)S(1)} %scatter-add.39), channel_id=1, source_target_pairs={{1,0},{2,1},{3,2},{4,3},{5,4},{6,5},{7,6},{8,7},{9,8},{10,9},{11,1... | collective-permute-start | bytes 786440 | tf_op jit(solution)/shard_map/ppermute | solution.py:20
  212.6 4.4 copy-start.15
  212.6 4.4 copy-start
  218.2 15.5 %collective-permute-start.7 = (f32[2,4,128,128]{3,2,1,0:T(8,128)S(1)}, f32[2,4,128,128]{3,2,1,0:T(8,128)S(1)}, u32[]{:S(2)}, u32[]{:S(2)}) collective-permute-start(f32[2,4,128,128]{3,2,1,0:T(8,128)S(1)} %pad_maximum_fusion.4), channel_id=1, source_target_pairs={{0,1},{1,2},{2,3},{3,4},{4,5},{5,6},{6,7},{7,8},{8,9},{9,10},{10,1... | collective-permute-start | bytes 1572872 | tf_op jit(solution)/shard_map/ppermute | solution.py:18
  224.4 15.3 %collective-permute-start.6 = (f32[2,4,128,128]{3,2,1,0:T(8,128)S(1)}, f32[2,4,128,128]{3,2,1,0:T(8,128)S(1)}, u32[]{:S(2)}, u32[]{:S(2)}) collective-permute-start(f32[2,4,128,128]{3,2,1,0:T(8,128)S(1)} %pad_maximum_fusion.4), channel_id=1, source_target_pairs={{1,0},{2,1},{3,2},{4,3},{5,4},{6,5},{7,6},{8,7},{9,8},{10,9},{11,1... | collective-permute-start | bytes 1572872 | tf_op jit(solution)/shard_map/ppermute | solution.py:20
  239.7 1.3 copy-start.5
  240.9 0.9 copy-start.11
  241.1 1.4 copy-start.3
  252.7 15.6 %collective-permute-start.9 = (f32[2,4,128,128]{3,2,1,0:T(8,128)S(1)}, f32[2,4,128,128]{3,2,1,0:T(8,128)S(1)}, u32[]{:S(2)}, u32[]{:S(2)}) collective-permute-start(f32[2,4,128,128]{3,2,1,0:T(8,128)S(1)} %pad_maximum_fusion.5), channel_id=1, source_target_pairs={{0,1},{1,2},{2,3},{3,4},{4,5},{5,6},{6,7},{7,8},{8,9},{9,10},{10,1... | collective-permute-start | bytes 1572872 | tf_op jit(solution)/shard_map/ppermute | solution.py:18
  258.3 13.0 %collective-permute-start.8 = (f32[2,4,128,128]{3,2,1,0:T(8,128)S(1)}, f32[2,4,128,128]{3,2,1,0:T(8,128)S(1)}, u32[]{:S(2)}, u32[]{:S(2)}) collective-permute-start(f32[2,4,128,128]{3,2,1,0:T(8,128)S(1)} %pad_maximum_fusion.5), channel_id=1, source_target_pairs={{1,0},{2,1},{3,2},{4,3},{5,4},{6,5},{7,6},{8,7},{9,8},{10,9},{11,1... | collective-permute-start | bytes 1572872 | tf_op jit(solution)/shard_map/ppermute | solution.py:20
  271.3 2.4 copy-start.4
  272.6 1.0 copy-start.6
  273.8 1.4 copy-start.2
  278.0 16.8 %collective-permute-start.11 = (f32[4,128,128]{2,1,0:T(8,128)S(1)}, f32[4,128,128]{2,1,0:T(8,128)}, u32[]{:S(2)}, u32[]{:S(2)}) collective-permute-start(f32[4,128,128]{2,1,0:T(8,128)S(1)} %scatter-add.53), channel_id=1, source_target_pairs={{0,1},{1,2},{2,3},{3,4},{4,5},{5,6},{6,7},{7,8},{8,9},{9,10},{10,1... | collective-permute-start | bytes 786440 | tf_op jit(solution)/shard_map/ppermute | solution.py:18
  284.9 9.9 %collective-permute-start.10 = (f32[4,128,128]{2,1,0:T(8,128)S(1)}, f32[4,128,128]{2,1,0:T(8,128)}, u32[]{:S(2)}, u32[]{:S(2)}) collective-permute-start(f32[4,128,128]{2,1,0:T(8,128)S(1)} %scatter-add.53), channel_id=1, source_target_pairs={{1,0},{2,1},{3,2},{4,3},{5,4},{6,5},{7,6},{8,7},{9,8},{10,9},{11,1... | collective-permute-start | bytes 786440 | tf_op jit(solution)/shard_map/ppermute | solution.py:20
  293.7 2.6 copy-start.8
  293.8 2.6 copy-start.10
  344.5 1.4 copy-start.1
Sparse Core Ops, SparseCore 0:
  9.5 90.0 all-gather.1
  346.0 97.5 reduce-scatter.1
